TPU v7x, 32 devices: a whole 2x2x4 slice. The times are simulated.
32 devices in a mesh: gx: 8 (over z, x), af: 4 (over y, core).
Axes of the slice: x: 2, y: 2, z: 4, core: 2. Of those that a mesh axis runs over, the one named last changes fastest.
Arguments:
- scalar_field: float32 [16, 512, 512], P('gx', 'af'), may hold values from -256 to 256
- plane_sketch: float32 [16, 2, 256], P('gx'), may hold values from -1.5 to 1.5
- second_sketch: float32 [512, 256], P('af'), may hold values from -0.25 to 0.25
- third_sketch: float32 [512, 256], replicated, may hold values from -0.25 to 0.25
- mixing: float32 [2, 256, 128], replicated, may hold values from -0.375 to 0.375
- plane_targets: int32 [16, 2], replicated, may hold values from 0 to 7
- plane_signs: int32 [16, 2], replicated, may hold values from 0 to 1
Outputs:
- factor_second: float32 [512, 128], P(('af', 'gx'))
- factor_third: float32 [512, 128], P(('gx', 'af'))
- core_sketch: float32 [128, 128, 128], P('gx', 'af')
Inputs may be any that keep to these rules, and one draw needn't show every extreme that they name: `plane_targets`: block id of each of a plane's two entries in the core sketch; the two may coincide. `plane_signs`: 1 stands for a plus sign, 0 for a minus sign.
All inputs are finite; a program needn't handle non-finite values.
Results may differ from a plain program's by a relative error of at most 0.0003.
Values sent between devices are 32-bit elements; how exact they have to be, the bound alone decides.
No kernel may reach another device: no remote copies, remote signals or barrier semaphores. Data moves between devices by JAX's collectives and lax.ppermute only.
A program may use at most 64 MiB of HBM per device.

v0:
```python
import functools

import jax
import jax.numpy as jnp
from jax import lax
from jax.experimental import pallas as pl
from jax.experimental.pallas import tpu as pltpu
from jax.sharding import PartitionSpec as P

BLOCK = 16
BLOCKS = 8
SUB = 8

precise = lax.Precision.HIGHEST
VMEM = pl.BlockSpec(memory_space=pltpu.VMEM)
SMEM = pl.BlockSpec(memory_space=pltpu.SMEM)
HBM = pl.BlockSpec(memory_space=pltpu.HBM)


def dot(left, right, dims):
    return lax.dot_general(
        left, right, (dims, ((), ())), precision=precise, preferred_element_type=jnp.float32
    )


def mm(left, right):
    return dot(left, right, ((1,), (0,)))


def mm_tn(left, right):
    return dot(left, right, ((0,), (0,)))


def mm_nt(left, right):
    return dot(left, right, ((1,), (1,)))


def inverse_lower(gram, tasks=()):
    size = gram.shape[0]
    count = size // SUB
    tasks = list(tasks)
    sub_ids = lax.broadcasted_iota(jnp.int32, (SUB, size), 0)
    lane_ids = lax.broadcasted_iota(jnp.int32, (SUB, size), 1)
    rows = [gram[SUB * i : SUB * i + SUB, :] for i in range(count)]
    done = []

    def along_sub(tile, j):
        return jnp.broadcast_to(tile[j : j + 1, :], (SUB, size))

    def along_lanes(tile, block):
        return [
            jnp.broadcast_to(tile[:, SUB * block + c : SUB * block + c + 1], (SUB, size))
            for c in range(SUB)
        ]

    diag = along_lanes(rows[0], 0)
    pivot = along_sub(diag[0], 0)
    for k in range(count):
        inside = (lane_ids >= SUB * k) & (lane_ids < SUB * k + SUB)
        cols = {i: along_lanes(rows[i], k) for i in range(k + 1, count)}
        ahead = along_lanes(rows[k + 1], k + 1) if k + 1 < count else None
        identity = jnp.where(lane_ids == sub_ids + SUB * k, 1.0, 0.0)
        rows[k] = jnp.where(inside, identity, rows[k])
        for i in range(k + 1, count):
            rows[i] = jnp.where(inside, 0.0, rows[i])
        pivots = None
        for j in range(SUB):
            pivots = pivot if j == 0 else jnp.where(sub_ids == j, pivot, pivots)
            scale = 1.0 / pivot
            heads = {c: along_sub(diag[c], j) for c in range(j + 1, SUB)}
            row_head = along_sub(rows[k], j)
            if j < SUB - 1:
                pivot = along_sub(diag[j + 1], j + 1) - (heads[j + 1] * heads[j + 1]) * scale
            elif k + 1 < count:
                head = along_sub(cols[k + 1][j], 0)
                pivot = along_sub(ahead[0], 0) - (head * head) * scale
            if j < SUB - 1:
                below = jnp.where(sub_ids > j, diag[j], 0.0)
                diag[j + 1] = diag[j + 1] - (below * heads[j + 1]) * scale
                factor = below * scale
                for c in range(j + 2, SUB):
                    diag[c] = diag[c] - factor * heads[c]
                rows[k] = rows[k] - factor * row_head
            for i in range(k + 1, count):
                factor = cols[i][j] * scale
                if i == k + 1:
                    for c in range(SUB):
                        ahead[c] = ahead[c] - factor * along_sub(cols[i][j], c)
                for c in range(j + 1, SUB):
                    cols[i][c] = cols[i][c] - factor * heads[c]
                rows[i] = rows[i] - factor * row_head
        kept = jnp.where(lane_ids < SUB * k + SUB, rows[k], 0.0)
        done.append(kept * lax.rsqrt(pivots))
        diag = ahead
        for task in tasks[: -(-len(tasks) // (count - k))]:
            task()
        tasks = tasks[-(-len(tasks) // (count - k)) :]
    return jnp.concatenate(done, axis=0)


def place():
    return [lax.axis_index(axis) for axis in ("gx", "ay", "ac")]


def third_sketch_kernel(
    gx, ay, field_in, plane_in, second_in, mixing_in, kept, given, *scratch
):
    field, plane_sketch, second_sketch, mixing, blocks, arrived = scratch
    copies = [
        pltpu.make_async_copy(source, target, arrived.at[n])
        for n, (source, target) in enumerate(
            (
                (plane_in, plane_sketch),
                (second_in, second_sketch),
                (mixing_in.at[1], mixing),
                (field_in, field),
            )
        )
    ]
    for copy in copies:
        copy.start()
    for copy in copies[:3]:
        copy.wait()
    planes, rows, cells = field.shape
    scaled = [second_sketch[...] * plane_sketch[p, 1:2, :] for p in range(planes)]
    weights = mm(jnp.concatenate(scaled, axis=0), mixing[...])
    copies[3].wait()
    wide = mm_tn(field[...].reshape(planes * rows, cells), weights)
    own = blocks.shape[2]
    for n in range(2 * gx * ay):
        blocks[n // (gx * ay), n % (gx * ay)] = wide[n * own : n * own + own, :]
    core = place()[2]
    blank = jnp.zeros((gx * ay, kept.shape[1] - own, kept.shape[2]), jnp.float32)
    for half, out in ((core, kept), (1 - core, given)):
        out[:, 0:own, :] = blocks[half]
        out[:, own:, :] = blank


def second_sketch_kernel(own, field, plane_sketch, third_sketch, mixing, out):
    planes, rows, cells = field.shape
    across = None
    for p in range(planes):
        term = mm(field[p], third_sketch[...] * plane_sketch[p, 0:1, :])
        across = term if across is None else across + term
    second = mm(across, mixing[0])
    strip = out.shape[1] - own
    for n in range(out.shape[0]):
        out[n, 0:own, :] = jnp.zeros((own, out.shape[2]), jnp.float32)
        out[n, own:, :] = second[n * strip : n * strip + strip, :]


def total_kernel(gx, ay, own, received, out):
    strip = received.shape[1] - own
    third = received[0, 0:own, :]
    for n in range(1, gx * ay):
        third = third + received[n, 0:own, :]
    seconds = []
    for y in range(ay):
        second = received[y, own:, :]
        for g in range(1, gx):
            second = second + received[g * ay + y, own:, :]
        seconds.append(second)
    for n in range(gx * ay):
        out[n, 0:own, :] = third
        for y in range(ay):
            out[n, own + y * strip : own + (y + 1) * strip, :] = seconds[y]


def core_ranges(gx, ay, own, ranges):
    strip = (ranges.shape[1] - own) // ay
    return [
        jnp.concatenate(
            [ranges[n, own + y * strip : own + (y + 1) * strip, :] for n in range(gx * ay)], axis=0
        )
        for y in range(ay)
    ]


def own_first(quarters):
    at = place()
    return jnp.concatenate(
        [
            jnp.where(at[1] == 0, quarters[0], quarters[1]),
            jnp.where(at[1] == 0, quarters[1], quarters[0]),
        ],
        axis=0,
    )


def same_core_kernel(gx, ay, own, ranges, near_field, far_field, product, gram):
    quarters = core_ranges(gx, ay, own, ranges)
    both = jnp.concatenate(quarters, axis=0)
    gram[...] = mm_tn(both, both)
    turned = jnp.transpose(own_first(quarters))
    cells = near_field.shape[2]
    for p in range(near_field.shape[0]):
        field = jnp.concatenate([near_field[p], far_field[p]], axis=0)
        product[:, p * cells : p * cells + cells] = mm(turned, field)


def second_kernel(
    gx, ay, ac, same, other, near_field, far_field, product, same_gram, inverse_out, partial, third
):
    at = place()
    planes, rows, cells = near_field.shape
    own = cells // (gx * ay * ac)
    rank = same.shape[2]
    quarters = core_ranges(gx, ay, own, other)
    both = jnp.concatenate(quarters, axis=0)
    gram = same_gram[...] + mm_tn(both, both)
    for swapped, ranges in enumerate((same, other)):
        for n in range(gx * ay):
            third[(at[2] ^ swapped) * (gx * ay) + n] = ranges[n, 0:own, :]
    all_third = jnp.concatenate([third[n] for n in range(gx * ay * ac)], axis=0)
    turned = jnp.transpose(own_first(quarters))
    halves = [[None, None] for _ in range(planes)]
    raw = [None] * planes
    width = cells // 2

    def field_product(p, h):
        span = slice(h * width, h * width + width)
        field = jnp.concatenate([near_field[p, :, span], far_field[p, :, span]], axis=0)
        held = product[:, p * cells + h * width : p * cells + h * width + width]
        halves[p][h] = held + mm(turned, field)

    def range_product(p):
        raw[p] = mm(jnp.concatenate(halves[p], axis=1), all_third)

    tasks = [functools.partial(field_product, p, h) for p in range(planes) for h in range(2)]
    tasks += [functools.partial(range_product, p) for p in range(planes)]
    inverse = inverse_lower(gram, tasks)
    inverse_out[...] = inverse
    share = rank // (ay * ac)
    own_rows = inverse[0:share, :]
    for a in range(1, ay * ac):
        piece = inverse[a * share : a * share + share, :]
        own_rows = jnp.where(at[1] * ac + at[2] == a, piece, own_rows)
    value = mm(own_rows, jnp.concatenate(raw, axis=1))
    for p in range(planes):
        for g in range(gx):
            partial[g, p] = value[:, p * rank : p * rank + rank]


def third_kernel(
    gx, ay, ac, own, targets, signs, same, other, second_inverse, *refs
):
    factor_second, factor_third, turned, weights, third = refs
    at = place()
    rank = same.shape[2]
    mine = core_ranges(gx, ay, own, same)
    mine = jnp.where(at[1] == 0, mine[0], mine[1]).reshape(gx, own, rank)
    own_range = mine[0]
    for g in range(1, gx):
        own_range = jnp.where(at[0] == g, mine[g], own_range)
    factor_second[...] = mm_nt(own_range, second_inverse[...])
    for swapped, ranges in enumerate((same, other)):
        for n in range(gx * ay):
            third[(at[2] ^ swapped) * (gx * ay) + n] = ranges[n, 0:own, :]
    all_third = jnp.concatenate([third[n] for n in range(gx * ay * ac)], axis=0)
    inverse = inverse_lower(mm_tn(all_third, all_third))
    turned[...] = jnp.transpose(inverse)
    factor_third[...] = mm_nt(third[(at[0] * ay + at[1]) * ac + at[2]], inverse)
    out_rows, turns, rank = weights.shape
    for r in range(out_rows):
        row = at[0] * out_rows + r
        for m in range(turns):
            plane = m * BLOCK + lax.rem(row, BLOCK)
            weight = jnp.float32(0)
            for t in range(targets.shape[1]):
                sign = (2 * signs[plane, t] - 1).astype(jnp.float32)
                weight = weight + jnp.where(targets[plane, t] == lax.div(row, BLOCK), sign, 0.0)
            weights[r, m : m + 1, :] = jnp.full((1, rank), weight, jnp.float32)


def core_kernel(weights, turned, planes, out):
    out_rows, turns, rank = weights.shape
    share = planes.shape[1]
    first = place()[0] * out_rows
    rows = []
    for r in range(out_rows):
        slot = r % BLOCK if out_rows % BLOCK == 0 else lax.rem(first + r, BLOCK)
        terms = [weights[r, m : m + 1, :] * planes[m * BLOCK + slot] for m in range(turns)]
        rows.append(sum(terms[1:], terms[0]))
    whole = mm(jnp.concatenate(rows, axis=0), turned[...])
    for r in range(out_rows):
        out[r] = whole[r * share : r * share + share, :]


def call(kernel, out_shapes, in_specs, flops, scratch=(), mib=48):
    return pl.pallas_call(
        kernel,
        out_shape=out_shapes,
        in_specs=in_specs,
        out_specs=jax.tree.map(lambda _: VMEM, out_shapes),
        scratch_shapes=scratch,
        compiler_params=pltpu.CompilerParams(vmem_limit_bytes=int(mib * 2**20)),
        cost_estimate=pl.CostEstimate(flops=flops, bytes_accessed=2**20, transcendentals=0),
    )


def in_hbm(source):
    return pltpu.with_memory_space_constraint(source, pltpu.HBM)


def swap(block, axis):
    perm = [(n, n ^ 1) for n in range(lax.axis_size(axis))]
    return lax.ppermute(block, axis, perm)


def body(
    scalar_field, plane_sketch, second_sketch, third_sketch, mixing, plane_targets, plane_signs
):
    gx, ay, ac = lax.axis_size("gx"), lax.axis_size("ay"), lax.axis_size("ac")
    planes, rows, cells = scalar_field.shape
    rank = mixing.shape[2]
    own = cells // (gx * ay * ac)
    strip = rows // (gx * ay)
    share = rank // (ay * ac)
    f32 = functools.partial(jax.ShapeDtypeStruct, dtype=jnp.float32)

    slot = f32((gx * ay, own + strip, rank))
    kept, given = call(
        functools.partial(third_sketch_kernel, gx, ay),
        [slot, slot],
        [HBM] * 4,
        10**9,
        [
            pltpu.VMEM(scalar_field.shape, jnp.float32),
            pltpu.VMEM(plane_sketch.shape, jnp.float32),
            pltpu.VMEM(second_sketch.shape, jnp.float32),
            pltpu.VMEM(mixing.shape[1:], jnp.float32),
            pltpu.VMEM((ac, gx * ay, own, rank), jnp.float32),
            pltpu.SemaphoreType.DMA((4,)),
        ],
    )(*(in_hbm(source) for source in (scalar_field, plane_sketch, second_sketch, mixing)))
    taken = swap(given, "ac")
    second = call(functools.partial(second_sketch_kernel, own), slot, [VMEM] * 4, 10**9)(
        scalar_field, plane_sketch, third_sketch, mixing
    )
    slots = kept + second + taken
    received = lax.all_to_all(slots, ("gx", "ay"), 0, 0, tiled=True)
    copies = call(
        functools.partial(total_kernel, gx, ay, own),
        f32((gx * ay, own + ay * strip, rank)),
        [VMEM],
        10**6,
    )(received)
    same = lax.all_to_all(copies, ("gx", "ay"), 0, 0, tiled=True)
    other = swap(same, "ac")
    across = swap(scalar_field, "ay")
    product, same_gram = call(
        functools.partial(same_core_kernel, gx, ay, own),
        [f32((rank, planes * cells)), f32((rank, rank))],
        [VMEM] * 3,
        10**9,
    )(same, scalar_field, across)
    second_inverse, partial = call(
        functools.partial(second_kernel, gx, ay, ac),
        [f32((rank, rank)), f32((gx, planes, share, rank))],
        [VMEM] * 6,
        2 * 10**9,
        [pltpu.VMEM((gx * ay * ac, own, rank), jnp.float32)],
    )(same, other, swap(scalar_field, "ac"), swap(across, "ac"), product, same_gram)
    every = lax.all_to_all(partial, "gx", 0, 0, tiled=True)
    out_rows = BLOCKS * BLOCK // gx
    factor_second, factor_third, turned, weights = call(
        functools.partial(third_kernel, gx, ay, ac, own),
        [
            f32((own, rank)),
            f32((own, rank)),
            f32((rank, rank)),
            f32((out_rows, gx * planes // BLOCK, rank)),
        ],
        [SMEM] * 2 + [VMEM] * 3,
        10**9,
        [pltpu.VMEM((gx * ay * ac, own, rank), jnp.float32)],
    )(plane_targets, plane_signs, same, other, second_inverse)
    core_sketch = call(core_kernel, f32((out_rows, share, rank)), [VMEM] * 3, 10**8)(
        weights, turned, every.reshape(gx * planes, share, rank)
    )
    return (factor_second, factor_third, core_sketch)


def solution(mesh):
    gx, af = mesh.devices.shape
    mesh = jax.sharding.Mesh(mesh.devices.reshape(gx, af // 2, 2), ("gx", "ay", "ac"))
    af = ("ay", "ac")
    in_specs = (P("gx", af, None), P("gx", None, None), P(af, None), P(), P(), P(), P())
    out_specs = (P(af + ("gx",), None), P(("gx",) + af, None), P("gx", af, None))
    return jax.shard_map(body, mesh=mesh, in_specs=in_specs, out_specs=out_specs, check_vma=False)
```

profile of v0, /device:TPU:0, one launch (start us, length us, event | category | flops | bytes accessed | tf_op | source)
XLA Modules:
  0.0 56.6 jit_solution(9313502366777107656)
XLA Ops:
  0.6 0.0 copy-start.2
  0.6 0.0 copy-start.1
  0.7 0.0 copy-start.3
  0.7 0.0 copy-start
  0.7 2.5 %shard_map.94 = (f32[16,24,128]{2,1,0:T(8,128)S(1)}, f32[16,24,128]{2,1,0:T(8,128)S(1)}) custom-call(f32[2,128,512]{2,1,0:T(8,128)} %near_field.1, f32[2,2,256]{2,1,0:T(2,128)} %plane_sketch.1, f32[128,256]{1,0:T(8,128)} %second_in.1, f32[2,256,128]{2,1,0:T(8,128)} %mixing.1), custom_call_target="tpu_custom_call" | custom-call | flops 1000000000 | bytes 1048576 | tf_op jit(solution)/shard_map/pallas_call | solution.py:322
  3.2 0.5 collective-permute-start
  3.7 0.0 copy-done.2
  3.7 0.0 copy-done.1
  3.7 0.0 copy-done.3
  3.7 0.0 copy-done
  3.7 1.1 %shard_map.95 = f32[16,24,128]{2,1,0:T(8,128)S(1)} custom-call(f32[2,128,512]{2,1,0:T(8,128)S(1)} %copy-done.1, f32[2,2,256]{2,1,0:T(2,128)S(1)} %copy-done.3, f32[512,256]{1,0:T(8,128)S(1)} %copy-done, f32[2,256,128]{2,1,0:T(8,128)S(1)} %copy-done.2), custom_call_target="tpu_custom_call" | custom-call | flops 1000000000 | bytes 1048576 | tf_op jit(solution)/shard_map/pallas_call | solution.py:337
  4.8 0.0 collective-permute-done
  4.9 0.7 %add_add_fusion = f32[16,24,128]{2,1,0:T(8,128)} fusion(f32[16,24,128]{2,1,0:T(8,128)S(1)} %collective-permute-done, f32[16,24,128]{2,1,0:T(8,128)S(1)} %get-tuple-element.13, f32[16,24,128]{2,1,0:T(8,128)S(1)} %shard_map.95), kind=kLoop, calls=%fused_computation | loop fusion | flops 98304 | bytes 786432 | tf_op jit(solution)/shard_map/add | solution.py:340
  5.6 8.2 %all-to-all-start = ((f32[16,24,128]{2,1,0:T(8,128)}), f32[16,24,128]{2,1,0:T(8,128)S(1)}, u32[]{:S(2)}, u32[]{:S(2)}) async-start(f32[16,24,128]{2,1,0:T(8,128)} %add_add_fusion), calls=%async_computation | async-start | bytes 393216 | tf_op jit(solution)/shard_map/all_to_all | solution.py:341
  13.7 1.9 %collective-permute-start.3 = (f32[2,128,512]{2,1,0:T(8,128)S(1)}, f32[2,128,512]{2,1,0:T(8,128)S(1)}, u32[]{:S(2)}, u32[]{:S(2)}) collective-permute-start(f32[2,128,512]{2,1,0:T(8,128)S(1)} %copy-done.1), channel_id=1, source_target_pairs={{0,2},{2,0},{1,3},{3,1},{4,6},{6,4},{5,7},{7,5},{8,10},{10,8},{9,1... | collective-permute-start | bytes 1572872 | tf_op jit(solution)/shard_map/ppermute | solution.py:307
  15.7 7.1 %all-to-all-done.received = f32[16,24,128]{2,1,0:T(8,128)S(1)} async-done(((f32[16,24,128]{2,1,0:T(8,128)}), f32[16,24,128]{2,1,0:T(8,128)S(1)}, u32[]{:S(2)}, u32[]{:S(2)}) %all-to-all-start) | async-done | bytes 196640 | tf_op jit(solution)/shard_map/all_to_all | solution.py:341
  22.8 0.7 %shard_map.96 = f32[16,32,128]{2,1,0:T(8,128)} custom-call(f32[16,24,128]{2,1,0:T(8,128)S(1)} %all-to-all-done.received), custom_call_target="tpu_custom_call" | custom-call | flops 1000000 | bytes 1048576 | tf_op jit(solution)/shard_map/pallas_call | solution.py:342
  23.5 3.5 %all-to-all-start.1 = ((f32[16,32,128]{2,1,0:T(8,128)}), f32[16,32,128]{2,1,0:T(8,128)S(1)}, u32[]{:S(2)}, u32[]{:S(2)}) async-start(f32[16,32,128]{2,1,0:T(8,128)} %shard_map.96), calls=%async_computation.1 | async-start | bytes 524288 | tf_op jit(solution)/shard_map/all_to_all | solution.py:348
  27.0 0.1 collective-permute-start.2
  27.1 2.8 %collective-permute-done.3.far_field = f32[2,128,512]{2,1,0:T(8,128)S(1)} collective-permute-done((f32[2,128,512]{2,1,0:T(8,128)S(1)}, f32[2,128,512]{2,1,0:T(8,128)S(1)}, u32[]{:S(2)}, u32[]{:S(2)}) %collective-permute-start.3) | collective-permute-done | bytes 524320 | tf_op jit(solution)/shard_map/ppermute | solution.py:307
  29.9 0.0 collective-permute-start.4
  29.9 6.5 %all-to-all-done.1.ranges.same = f32[16,32,128]{2,1,0:T(8,128)S(1)} async-done(((f32[16,32,128]{2,1,0:T(8,128)}), f32[16,32,128]{2,1,0:T(8,128)S(1)}, u32[]{:S(2)}, u32[]{:S(2)}) %all-to-all-start.1) | async-done | bytes 262176 | tf_op jit(solution)/shard_map/all_to_all | solution.py:348
  36.3 0.0 collective-permute-start.1
  36.4 0.8 %shard_map.97 = (f32[128,1024]{1,0:T(8,128)S(1)}, f32[128,128]{1,0:T(8,128)S(1)}) custom-call(f32[16,32,128]{2,1,0:T(8,128)S(1)} %all-to-all-done.1.ranges.same, f32[2,128,512]{2,1,0:T(8,128)S(1)} %copy-done.1, f32[2,128,512]{2,1,0:T(8,128)S(1)} %collective-permute-done.3.far_field), custom_call_target="tpu_custom_call" | custom-call | flops 1000000000 | bytes 1048576 | tf_op jit(solution)/shard_map/pallas_call | solution.py:351
  37.1 0.0 collective-permute-done.2.near_field
  37.1 0.0 collective-permute-done.4.far_field
  37.1 0.7 %collective-permute-done.1.other = f32[16,32,128]{2,1,0:T(8,128)S(1)} collective-permute-done((f32[16,32,128]{2,1,0:T(8,128)S(1)}, f32[16,32,128]{2,1,0:T(8,128)S(1)}, u32[]{:S(2)}, u32[]{:S(2)}) %collective-permute-start.1) | collective-permute-done | bytes 262176 | tf_op jit(solution)/shard_map/ppermute | solution.py:307
  37.9 4.7 %shard_map.98 = (f32[128,128]{1,0:T(8,128)S(1)}, f32[8,2,32,128]{3,2,1,0:T(8,128)}) custom-call(f32[16,32,128]{2,1,0:T(8,128)S(1)} %all-to-all-done.1.ranges.same, f32[16,32,128]{2,1,0:T(8,128)S(1)} %collective-permute-done.1.other, f32[2,128,512]{2,1,0:T(8,128)S(1)} %collective-permute-done.2.near_field, ...), custom_call_target="tpu_custom_call" | custom-call | flops 2000000000 | bytes 1048576 | tf_op jit(solution)/shard_map/pallas_call | solution.py:357
  42.6 0.0 copy-start.4
  42.6 3.6 %all-to-all-start.2 = ((f32[8,2,32,128]{3,2,1,0:T(8,128)}), f32[8,2,32,128]{3,2,1,0:T(8,128)S(1)}, u32[]{:S(2)}, u32[]{:S(2)}) async-start(f32[8,2,32,128]{3,2,1,0:T(8,128)} %get-tuple-element.22), calls=%async_computation.2 | async-start | bytes 524288 | tf_op jit(solution)/shard_map/all_to_all | solution.py:364
  46.2 0.0 copy-done.4
  46.2 0.0 copy-start.5
  46.2 0.1 copy.10.targets
  46.3 0.6 %copy-done.5 = s32[16,2]{0,1:T(2,128)S(1)} copy-done((s32[16,2]{0,1:T(2,128)S(1)}, s32[16,2]{0,1:T(2,128)}, u32[]{:S(2)}) %copy-start.5) | copy-done | bytes 152
  46.8 0.1 copy.11.signs
  46.9 5.1 %shard_map.99 = (f32[16,128]{1,0:T(8,128)}, f32[16,128]{1,0:T(8,128)}, f32[128,128]{1,0:T(8,128)S(1)}, f32[16,1,128]{2,1,0:T(1,128)S(1)}) custom-call(s32[16,2]{1,0:T(8,128)S(1)} %copy.10.targets, s32[16,2]{1,0:T(8,128)S(1)} %copy.11.signs, f32[16,32,128]{2,1,0:T(8,128)S(1)} %all-to-all-done.1.ranges.same, f32[16,32,128]{2,1,0:T(8,128)S(1)} %collective-permute-done.1.other, ...), custom_call_target="tpu_custom_call" | custom-call | flops 1000000000 | bytes 1048576 | tf_op jit(solution)/shard_map/pallas_call | solution.py:366
  52.1 3.5 %all-to-all-done.2 = f32[8,2,32,128]{3,2,1,0:T(8,128)S(1)} async-done(((f32[8,2,32,128]{3,2,1,0:T(8,128)}), f32[8,2,32,128]{3,2,1,0:T(8,128)S(1)}, u32[]{:S(2)}, u32[]{:S(2)}) %all-to-all-start.2) | async-done | bytes 262176 | tf_op jit(solution)/shard_map/all_to_all | solution.py:364
  55.6 1.1 %shard_map.100 = f32[16,32,128]{2,1,0:T(8,128)} custom-call(f32[16,1,128]{2,1,0:T(1,128)S(1)} %get-tuple-element.20.weights, f32[128,128]{1,0:T(8,128)S(1)} %get-tuple-element.21.turned, f32[16,32,128]{2,1,0:T(8,128)S(1)} %bitcast.1), custom_call_target="tpu_custom_call" | custom-call | flops 100000000 | bytes 1048576 | tf_op jit(solution)/shard_map/pallas_call | solution.py:378
Async XLA Ops:
  0.6 3.1 %copy-start.2 = (f32[2,256,128]{2,1,0:T(8,128)S(1)}, f32[2,256,128]{2,1,0:T(8,128)}, u32[]{:S(2)}) copy-start(f32[2,256,128]{2,1,0:T(8,128)} %mixing.1) | copy-start | bytes 786436
  0.6 3.1 %copy-start.1 = (f32[2,128,512]{2,1,0:T(8,128)S(1)}, f32[2,128,512]{2,1,0:T(8,128)}, u32[]{:S(2)}) copy-start(f32[2,128,512]{2,1,0:T(8,128)} %near_field.1) | copy-start | bytes 1572868
  0.7 3.1 %copy-start.3 = (f32[2,2,256]{2,1,0:T(2,128)S(1)}, f32[2,2,256]{2,1,0:T(2,128)}, u32[]{:S(2)}) copy-start(f32[2,2,256]{2,1,0:T(2,128)} %plane_sketch.1) | copy-start | bytes 12292
  0.7 3.1 %copy-start = (f32[512,256]{1,0:T(8,128)S(1)}, f32[512,256]{1,0:T(8,128)}, u32[]{:S(2)}) copy-start(f32[512,256]{1,0:T(8,128)} %third_sketch.1) | copy-start | bytes 1572868
  3.2 1.7 %collective-permute-start = (f32[16,24,128]{2,1,0:T(8,128)S(1)}, f32[16,24,128]{2,1,0:T(8,128)S(1)}, u32[]{:S(2)}, u32[]{:S(2)}) collective-permute-start(f32[16,24,128]{2,1,0:T(8,128)S(1)} %get-tuple-element.14), channel_id=1, source_target_pairs={{0,1},{1,0},{2,3},{3,2},{4,5},{5,4},{6,7},{7,6},{8,9},{9,8},{10,11... | collective-permute-start | bytes 589832 | tf_op jit(solution)/shard_map/ppermute | solution.py:307
  5.6 17.2 %all-to-all-start = ((f32[16,24,128]{2,1,0:T(8,128)}), f32[16,24,128]{2,1,0:T(8,128)S(1)}, u32[]{:S(2)}, u32[]{:S(2)}) async-start(f32[16,24,128]{2,1,0:T(8,128)} %add_add_fusion), calls=%async_computation | async-start | bytes 393216 | tf_op jit(solution)/shard_map/all_to_all | solution.py:341
  13.7 16.2 %collective-permute-start.3 = (f32[2,128,512]{2,1,0:T(8,128)S(1)}, f32[2,128,512]{2,1,0:T(8,128)S(1)}, u32[]{:S(2)}, u32[]{:S(2)}) collective-permute-start(f32[2,128,512]{2,1,0:T(8,128)S(1)} %copy-done.1), channel_id=1, source_target_pairs={{0,2},{2,0},{1,3},{3,1},{4,6},{6,4},{5,7},{7,5},{8,10},{10,8},{9,1... | collective-permute-start | bytes 1572872 | tf_op jit(solution)/shard_map/ppermute | solution.py:307
  23.5 12.9 %all-to-all-start.1 = ((f32[16,32,128]{2,1,0:T(8,128)}), f32[16,32,128]{2,1,0:T(8,128)S(1)}, u32[]{:S(2)}, u32[]{:S(2)}) async-start(f32[16,32,128]{2,1,0:T(8,128)} %shard_map.96), calls=%async_computation.1 | async-start | bytes 524288 | tf_op jit(solution)/shard_map/all_to_all | solution.py:348
  27.0 10.1 %collective-permute-start.2 = (f32[2,128,512]{2,1,0:T(8,128)S(1)}, f32[2,128,512]{2,1,0:T(8,128)S(1)}, u32[]{:S(2)}, u32[]{:S(2)}) collective-permute-start(f32[2,128,512]{2,1,0:T(8,128)S(1)} %copy-done.1), channel_id=1, source_target_pairs={{0,1},{1,0},{2,3},{3,2},{4,5},{5,4},{6,7},{7,6},{8,9},{9,8},{10,11... | collective-permute-start | bytes 1572872 | tf_op jit(solution)/shard_map/ppermute | solution.py:307
  29.9 7.2 %collective-permute-start.4 = (f32[2,128,512]{2,1,0:T(8,128)S(1)}, f32[2,128,512]{2,1,0:T(8,128)S(1)}, u32[]{:S(2)}, u32[]{:S(2)}) collective-permute-start(f32[2,128,512]{2,1,0:T(8,128)S(1)} %collective-permute-done.3.far_field), channel_id=1, source_target_pairs={{0,1},{1,0},{2,3},{3,2},{4,5},{5,4},{6,7},{7,6},{8,9},{9,8},{10,11... | collective-permute-start | bytes 1572872 | tf_op jit(solution)/shard_map/ppermute | solution.py:307
  36.3 1.5 %collective-permute-start.1 = (f32[16,32,128]{2,1,0:T(8,128)S(1)}, f32[16,32,128]{2,1,0:T(8,128)S(1)}, u32[]{:S(2)}, u32[]{:S(2)}) collective-permute-start(f32[16,32,128]{2,1,0:T(8,128)S(1)} %all-to-all-done.1.ranges.same), channel_id=1, source_target_pairs={{0,1},{1,0},{2,3},{3,2},{4,5},{5,4},{6,7},{7,6},{8,9},{9,8},{10,11... | collective-permute-start | bytes 786440 | tf_op jit(solution)/shard_map/ppermute | solution.py:307
  42.6 3.6 %copy-start.4 = (s32[16,2]{0,1:T(2,128)S(1)}, s32[16,2]{0,1:T(2,128)}, u32[]{:S(2)}) copy-start(s32[16,2]{0,1:T(2,128)} %param.12) | copy-start | bytes 388
  42.6 13.0 %all-to-all-start.2 = ((f32[8,2,32,128]{3,2,1,0:T(8,128)}), f32[8,2,32,128]{3,2,1,0:T(8,128)S(1)}, u32[]{:S(2)}, u32[]{:S(2)}) async-start(f32[8,2,32,128]{3,2,1,0:T(8,128)} %get-tuple-element.22), calls=%async_computation.2 | async-start | bytes 524288 | tf_op jit(solution)/shard_map/all_to_all | solution.py:364
  46.2 0.7 %copy-start.5 = (s32[16,2]{0,1:T(2,128)S(1)}, s32[16,2]{0,1:T(2,128)}, u32[]{:S(2)}) copy-start(s32[16,2]{0,1:T(2,128)} %param.13) | copy-start | bytes 388
where the time goes:
time: 57.1 us; the launch traced here: 56.6 us
  waiting for transfers between devices  20.6 us (36%)
  starting transfers between devices  17.8 us (31%)
  Pallas kernels  16 us (28%)
  local copies, waits for them, and re-layouts  0.78 us (1%)
  between operations  0.75 us (1%)
  other arithmetic  0.71 us (1%)
    all_to_all x1, starting transfers between devices, body(): received = lax.all_to_all(slots, ('gx', 'ay'), 0, 0, tiled=True)  8.15 us
    all_to_all x1, waiting for transfers between devices, body(): received = lax.all_to_all(slots, ('gx', 'ay'), 0, 0, tiled=True)  7.09 us
    all_to_all x1, waiting for transfers between devices, body(): same = lax.all_to_all(copies, ('gx', 'ay'), 0, 0, tiled=True)  6.45 us
    pallas_call x1, Pallas kernels, body(): call(functools.partial(third_kernel, gx, ay, ac, own), [f32((own, rank)),...  5.13 us
    pallas_call x1, Pallas kernels, body(): call(functools.partial(second_kernel, gx, ay, ac), [f32((rank, rank)), f3...  4.7 us
    all_to_all x1, starting transfers between devices, body(): every = lax.all_to_all(partial, 'gx', 0, 0, tiled=True)  3.57 us
    all_to_all x1, starting transfers between devices, body(): same = lax.all_to_all(copies, ('gx', 'ay'), 0, 0, tiled=True)  3.53 us
    ppermute x5, waiting for transfers between devices, swap(): return lax.ppermute(block, axis, perm)  3.53 us
  transfers between devices with their start and end apart: 8, of which 5 were waited for; matrix products, arithmetic and copies ran while one was open for 0% of the time, Pallas kernels for 14%

commit v1 on v0

--- a/solution.py
+++ b/solution.py
@@ -57,7 +57,10 @@
     pivot = along_sub(diag[0], 0)
     for k in range(count):
         inside = (lane_ids >= SUB * k) & (lane_ids < SUB * k + SUB)
-        cols = {i: along_lanes(rows[i], k) for i in range(k + 1, count)}
+        cols = {i: along_lanes(rows[i], k) for i in range(k + 2, count)}
+        if k + 1 < count:
+            cols[k + 1] = along_lanes(rows[1], 0) if k == 0 else below_next
+        below_next = along_lanes(rows[k + 2], k + 1) if k + 2 < count else None
         ahead = along_lanes(rows[k + 1], k + 1) if k + 1 < count else None
         identity = jnp.where(lane_ids == sub_ids + SUB * k, 1.0, 0.0)
         rows[k] = jnp.where(inside, identity, rows[k])
@@ -84,8 +87,12 @@
             for i in range(k + 1, count):
                 factor = cols[i][j] * scale
                 if i == k + 1:
+                    next_heads = [along_sub(cols[i][j], c) for c in range(SUB)]
                     for c in range(SUB):
-                        ahead[c] = ahead[c] - factor * along_sub(cols[i][j], c)
+                        ahead[c] = ahead[c] - factor * next_heads[c]
+                if i == k + 2:
+                    for c in range(SUB):
+                        below_next[c] = below_next[c] - factor * next_heads[c]
                 for c in range(j + 1, SUB):
                     cols[i][c] = cols[i][c] - factor * heads[c]
                 rows[i] = rows[i] - factor * row_head
@@ -125,7 +132,7 @@
     scaled = [second_sketch[...] * plane_sketch[p, 1:2, :] for p in range(planes)]
     weights = mm(jnp.concatenate(scaled, axis=0), mixing[...])
     copies[3].wait()
-    wide = mm_tn(field[...].reshape(planes * rows, cells), weights)
+    wide = jnp.transpose(mm_tn(weights, field[...].reshape(planes * rows, cells)))
     own = blocks.shape[2]
     for n in range(2 * gx * ay):
         blocks[n // (gx * ay), n % (gx * ay)] = wide[n * own : n * own + own, :]

time: 57.1 us -> 56.9 us (level)
  transfers between devices with their start and end apart: 8 -> 8, of which waited for: 5 -> 5; matrix products, arithmetic and copies ran while one was open for 0% -> 0% of each run, Pallas kernels for 14% -> 13%
where the time goes in v1:
time: 56.9 us; the launch traced here: 56.4 us
  waiting for transfers between devices  20.8 us (37%)
  starting transfers between devices  17.8 us (31%)
  Pallas kernels  15.6 us (27%)
  local copies, waits for them, and re-layouts  0.78 us (1%)
  between operations  0.75 us (1%)
  other arithmetic  0.71 us (1%)
    all_to_all x1, starting transfers between devices, body(): received = lax.all_to_all(slots, ('gx', 'ay'), 0, 0, tiled=True)  8.16 us
    all_to_all x1, waiting for transfers between devices, body(): received = lax.all_to_all(slots, ('gx', 'ay'), 0, 0, tiled=True)  7.09 us
    all_to_all x1, waiting for transfers between devices, body(): same = lax.all_to_all(copies, ('gx', 'ay'), 0, 0, tiled=True)  6.45 us
    pallas_call x1, Pallas kernels, body(): call(functools.partial(third_kernel, gx, ay, ac, own), [f32((own, rank)),...  4.9 us
    pallas_call x1, Pallas kernels, body(): call(functools.partial(second_kernel, gx, ay, ac), [f32((rank, rank)), f3...  4.64 us
    all_to_all x1, waiting for transfers between devices, body(): every = lax.all_to_all(partial, 'gx', 0, 0, tiled=True)  3.74 us
    all_to_all x1, starting transfers between devices, body(): every = lax.all_to_all(partial, 'gx', 0, 0, tiled=True)  3.57 us
    all_to_all x1, starting transfers between devices, body(): same = lax.all_to_all(copies, ('gx', 'ay'), 0, 0, tiled=True)  3.53 us
  transfers between devices with their start and end apart: 8, of which 5 were waited for; matrix products, arithmetic and copies ran while one was open for 0% of the time, Pallas kernels for 13%

profile of v1, /device:TPU:0, one launch (start us, length us, event | category | flops | bytes accessed | tf_op | source)
XLA Modules:
  0.0 56.4 jit_solution(8147761125137281564)
XLA Ops:
  0.6 0.0 copy-start.2
  0.6 0.0 copy-start.1
  0.7 0.0 copy-start.3
  0.7 0.0 copy-start
  0.7 2.4 %shard_map.94 = (f32[16,24,128]{2,1,0:T(8,128)S(1)}, f32[16,24,128]{2,1,0:T(8,128)S(1)}) custom-call(f32[2,128,512]{2,1,0:T(8,128)} %near_field.1, f32[2,2,256]{2,1,0:T(2,128)} %plane_sketch.1, f32[128,256]{1,0:T(8,128)} %second_in.1, f32[2,256,128]{2,1,0:T(8,128)} %mixing.1), custom_call_target="tpu_custom_call" | custom-call | flops 1000000000 | bytes 1048576 | tf_op jit(solution)/shard_map/pallas_call | solution.py:329
  3.1 0.5 collective-permute-start
  3.6 0.0 copy-done.2
  3.6 0.0 copy-done.1
  3.6 0.0 copy-done.3
  3.6 0.0 copy-done
  3.6 1.1 %shard_map.95 = f32[16,24,128]{2,1,0:T(8,128)S(1)} custom-call(f32[2,128,512]{2,1,0:T(8,128)S(1)} %copy-done.1, f32[2,2,256]{2,1,0:T(2,128)S(1)} %copy-done.3, f32[512,256]{1,0:T(8,128)S(1)} %copy-done, f32[2,256,128]{2,1,0:T(8,128)S(1)} %copy-done.2), custom_call_target="tpu_custom_call" | custom-call | flops 1000000000 | bytes 1048576 | tf_op jit(solution)/shard_map/pallas_call | solution.py:344
  4.7 0.0 collective-permute-done
  4.7 0.7 %add_add_fusion = f32[16,24,128]{2,1,0:T(8,128)} fusion(f32[16,24,128]{2,1,0:T(8,128)S(1)} %collective-permute-done, f32[16,24,128]{2,1,0:T(8,128)S(1)} %get-tuple-element.13, f32[16,24,128]{2,1,0:T(8,128)S(1)} %shard_map.95), kind=kLoop, calls=%fused_computation | loop fusion | flops 98304 | bytes 786432 | tf_op jit(solution)/shard_map/add | solution.py:347
  5.4 8.2 %all-to-all-start = ((f32[16,24,128]{2,1,0:T(8,128)}), f32[16,24,128]{2,1,0:T(8,128)S(1)}, u32[]{:S(2)}, u32[]{:S(2)}) async-start(f32[16,24,128]{2,1,0:T(8,128)} %add_add_fusion), calls=%async_computation | async-start | bytes 393216 | tf_op jit(solution)/shard_map/all_to_all | solution.py:348
  13.6 1.9 %collective-permute-start.3 = (f32[2,128,512]{2,1,0:T(8,128)S(1)}, f32[2,128,512]{2,1,0:T(8,128)S(1)}, u32[]{:S(2)}, u32[]{:S(2)}) collective-permute-start(f32[2,128,512]{2,1,0:T(8,128)S(1)} %copy-done.1), channel_id=1, source_target_pairs={{0,2},{2,0},{1,3},{3,1},{4,6},{6,4},{5,7},{7,5},{8,10},{10,8},{9,1... | collective-permute-start | bytes 1572872 | tf_op jit(solution)/shard_map/ppermute | solution.py:314
  15.5 7.1 %all-to-all-done.received = f32[16,24,128]{2,1,0:T(8,128)S(1)} async-done(((f32[16,24,128]{2,1,0:T(8,128)}), f32[16,24,128]{2,1,0:T(8,128)S(1)}, u32[]{:S(2)}, u32[]{:S(2)}) %all-to-all-start) | async-done | bytes 196640 | tf_op jit(solution)/shard_map/all_to_all | solution.py:348
  22.6 0.7 %shard_map.96 = f32[16,32,128]{2,1,0:T(8,128)} custom-call(f32[16,24,128]{2,1,0:T(8,128)S(1)} %all-to-all-done.received), custom_call_target="tpu_custom_call" | custom-call | flops 1000000 | bytes 1048576 | tf_op jit(solution)/shard_map/pallas_call | solution.py:349
  23.3 3.5 %all-to-all-start.1 = ((f32[16,32,128]{2,1,0:T(8,128)}), f32[16,32,128]{2,1,0:T(8,128)S(1)}, u32[]{:S(2)}, u32[]{:S(2)}) async-start(f32[16,32,128]{2,1,0:T(8,128)} %shard_map.96), calls=%async_computation.1 | async-start | bytes 524288 | tf_op jit(solution)/shard_map/all_to_all | solution.py:355
  26.9 0.1 collective-permute-start.2
  27.0 2.8 %collective-permute-done.3.far_field = f32[2,128,512]{2,1,0:T(8,128)S(1)} collective-permute-done((f32[2,128,512]{2,1,0:T(8,128)S(1)}, f32[2,128,512]{2,1,0:T(8,128)S(1)}, u32[]{:S(2)}, u32[]{:S(2)}) %collective-permute-start.3) | collective-permute-done | bytes 524320 | tf_op jit(solution)/shard_map/ppermute | solution.py:314
  29.8 0.0 collective-permute-start.4
  29.8 6.5 %all-to-all-done.1.ranges.same = f32[16,32,128]{2,1,0:T(8,128)S(1)} async-done(((f32[16,32,128]{2,1,0:T(8,128)}), f32[16,32,128]{2,1,0:T(8,128)S(1)}, u32[]{:S(2)}, u32[]{:S(2)}) %all-to-all-start.1) | async-done | bytes 262176 | tf_op jit(solution)/shard_map/all_to_all | solution.py:355
  36.2 0.0 collective-permute-start.1
  36.2 0.8 %shard_map.97 = (f32[128,1024]{1,0:T(8,128)S(1)}, f32[128,128]{1,0:T(8,128)S(1)}) custom-call(f32[16,32,128]{2,1,0:T(8,128)S(1)} %all-to-all-done.1.ranges.same, f32[2,128,512]{2,1,0:T(8,128)S(1)} %copy-done.1, f32[2,128,512]{2,1,0:T(8,128)S(1)} %collective-permute-done.3.far_field), custom_call_target="tpu_custom_call" | custom-call | flops 1000000000 | bytes 1048576 | tf_op jit(solution)/shard_map/pallas_call | solution.py:358
  37.0 0.0 collective-permute-done.2.near_field
  37.0 0.0 collective-permute-done.4.far_field
  37.0 0.7 %collective-permute-done.1.other = f32[16,32,128]{2,1,0:T(8,128)S(1)} collective-permute-done((f32[16,32,128]{2,1,0:T(8,128)S(1)}, f32[16,32,128]{2,1,0:T(8,128)S(1)}, u32[]{:S(2)}, u32[]{:S(2)}) %collective-permute-start.1) | collective-permute-done | bytes 262176 | tf_op jit(solution)/shard_map/ppermute | solution.py:314
  37.7 4.6 %shard_map.98 = (f32[128,128]{1,0:T(8,128)S(1)}, f32[8,2,32,128]{3,2,1,0:T(8,128)}) custom-call(f32[16,32,128]{2,1,0:T(8,128)S(1)} %all-to-all-done.1.ranges.same, f32[16,32,128]{2,1,0:T(8,128)S(1)} %collective-permute-done.1.other, f32[2,128,512]{2,1,0:T(8,128)S(1)} %collective-permute-done.2.near_field, ...), custom_call_target="tpu_custom_call" | custom-call | flops 2000000000 | bytes 1048576 | tf_op jit(solution)/shard_map/pallas_call | solution.py:364
  42.4 0.0 copy-start.4
  42.4 3.6 %all-to-all-start.2 = ((f32[8,2,32,128]{3,2,1,0:T(8,128)}), f32[8,2,32,128]{3,2,1,0:T(8,128)S(1)}, u32[]{:S(2)}, u32[]{:S(2)}) async-start(f32[8,2,32,128]{3,2,1,0:T(8,128)} %get-tuple-element.22), calls=%async_computation.2 | async-start | bytes 524288 | tf_op jit(solution)/shard_map/all_to_all | solution.py:371
  46.0 0.0 copy-done.4
  46.0 0.0 copy-start.5
  46.0 0.1 copy.10.targets
  46.1 0.6 %copy-done.5 = s32[16,2]{0,1:T(2,128)S(1)} copy-done((s32[16,2]{0,1:T(2,128)S(1)}, s32[16,2]{0,1:T(2,128)}, u32[]{:S(2)}) %copy-start.5) | copy-done | bytes 152
  46.6 0.1 copy.11.signs
  46.7 4.9 %shard_map.99 = (f32[16,128]{1,0:T(8,128)}, f32[16,128]{1,0:T(8,128)}, f32[128,128]{1,0:T(8,128)S(1)}, f32[16,1,128]{2,1,0:T(1,128)S(1)}) custom-call(s32[16,2]{1,0:T(8,128)S(1)} %copy.10.targets, s32[16,2]{1,0:T(8,128)S(1)} %copy.11.signs, f32[16,32,128]{2,1,0:T(8,128)S(1)} %all-to-all-done.1.ranges.same, f32[16,32,128]{2,1,0:T(8,128)S(1)} %collective-permute-done.1.other, ...), custom_call_target="tpu_custom_call" | custom-call | flops 1000000000 | bytes 1048576 | tf_op jit(solution)/shard_map/pallas_call | solution.py:373
  51.6 3.7 %all-to-all-done.2 = f32[8,2,32,128]{3,2,1,0:T(8,128)S(1)} async-done(((f32[8,2,32,128]{3,2,1,0:T(8,128)}), f32[8,2,32,128]{3,2,1,0:T(8,128)S(1)}, u32[]{:S(2)}, u32[]{:S(2)}) %all-to-all-start.2) | async-done | bytes 262176 | tf_op jit(solution)/shard_map/all_to_all | solution.py:371
  55.4 1.1 %shard_map.100 = f32[16,32,128]{2,1,0:T(8,128)} custom-call(f32[16,1,128]{2,1,0:T(1,128)S(1)} %get-tuple-element.20.weights, f32[128,128]{1,0:T(8,128)S(1)} %get-tuple-element.21.turned, f32[16,32,128]{2,1,0:T(8,128)S(1)} %bitcast.1), custom_call_target="tpu_custom_call" | custom-call | flops 100000000 | bytes 1048576 | tf_op jit(solution)/shard_map/pallas_call | solution.py:385
Async XLA Ops:
  0.6 2.9 %copy-start.2 = (f32[2,256,128]{2,1,0:T(8,128)S(1)}, f32[2,256,128]{2,1,0:T(8,128)}, u32[]{:S(2)}) copy-start(f32[2,256,128]{2,1,0:T(8,128)} %mixing.1) | copy-start | bytes 786436
  0.6 2.9 %copy-start.1 = (f32[2,128,512]{2,1,0:T(8,128)S(1)}, f32[2,128,512]{2,1,0:T(8,128)}, u32[]{:S(2)}) copy-start(f32[2,128,512]{2,1,0:T(8,128)} %near_field.1) | copy-start | bytes 1572868
  0.7 2.9 %copy-start.3 = (f32[2,2,256]{2,1,0:T(2,128)S(1)}, f32[2,2,256]{2,1,0:T(2,128)}, u32[]{:S(2)}) copy-start(f32[2,2,256]{2,1,0:T(2,128)} %plane_sketch.1) | copy-start | bytes 12292
  0.7 2.9 %copy-start = (f32[512,256]{1,0:T(8,128)S(1)}, f32[512,256]{1,0:T(8,128)}, u32[]{:S(2)}) copy-start(f32[512,256]{1,0:T(8,128)} %third_sketch.1) | copy-start | bytes 1572868
  3.1 1.7 %collective-permute-start = (f32[16,24,128]{2,1,0:T(8,128)S(1)}, f32[16,24,128]{2,1,0:T(8,128)S(1)}, u32[]{:S(2)}, u32[]{:S(2)}) collective-permute-start(f32[16,24,128]{2,1,0:T(8,128)S(1)} %get-tuple-element.14), channel_id=1, source_target_pairs={{0,1},{1,0},{2,3},{3,2},{4,5},{5,4},{6,7},{7,6},{8,9},{9,8},{10,11... | collective-permute-start | bytes 589832 | tf_op jit(solution)/shard_map/ppermute | solution.py:314
  5.4 17.2 %all-to-all-start = ((f32[16,24,128]{2,1,0:T(8,128)}), f32[16,24,128]{2,1,0:T(8,128)S(1)}, u32[]{:S(2)}, u32[]{:S(2)}) async-start(f32[16,24,128]{2,1,0:T(8,128)} %add_add_fusion), calls=%async_computation | async-start | bytes 393216 | tf_op jit(solution)/shard_map/all_to_all | solution.py:348
  13.6 16.2 %collective-permute-start.3 = (f32[2,128,512]{2,1,0:T(8,128)S(1)}, f32[2,128,512]{2,1,0:T(8,128)S(1)}, u32[]{:S(2)}, u32[]{:S(2)}) collective-permute-start(f32[2,128,512]{2,1,0:T(8,128)S(1)} %copy-done.1), channel_id=1, source_target_pairs={{0,2},{2,0},{1,3},{3,1},{4,6},{6,4},{5,7},{7,5},{8,10},{10,8},{9,1... | collective-permute-start | bytes 1572872 | tf_op jit(solution)/shard_map/ppermute | solution.py:314
  23.3 12.9 %all-to-all-start.1 = ((f32[16,32,128]{2,1,0:T(8,128)}), f32[16,32,128]{2,1,0:T(8,128)S(1)}, u32[]{:S(2)}, u32[]{:S(2)}) async-start(f32[16,32,128]{2,1,0:T(8,128)} %shard_map.96), calls=%async_computation.1 | async-start | bytes 524288 | tf_op jit(solution)/shard_map/all_to_all | solution.py:355
  26.9 10.1 %collective-permute-start.2 = (f32[2,128,512]{2,1,0:T(8,128)S(1)}, f32[2,128,512]{2,1,0:T(8,128)S(1)}, u32[]{:S(2)}, u32[]{:S(2)}) collective-permute-start(f32[2,128,512]{2,1,0:T(8,128)S(1)} %copy-done.1), channel_id=1, source_target_pairs={{0,1},{1,0},{2,3},{3,2},{4,5},{5,4},{6,7},{7,6},{8,9},{9,8},{10,11... | collective-permute-start | bytes 1572872 | tf_op jit(solution)/shard_map/ppermute | solution.py:314
  29.8 7.2 %collective-permute-start.4 = (f32[2,128,512]{2,1,0:T(8,128)S(1)}, f32[2,128,512]{2,1,0:T(8,128)S(1)}, u32[]{:S(2)}, u32[]{:S(2)}) collective-permute-start(f32[2,128,512]{2,1,0:T(8,128)S(1)} %collective-permute-done.3.far_field), channel_id=1, source_target_pairs={{0,1},{1,0},{2,3},{3,2},{4,5},{5,4},{6,7},{7,6},{8,9},{9,8},{10,11... | collective-permute-start | bytes 1572872 | tf_op jit(solution)/shard_map/ppermute | solution.py:314
  36.2 1.5 %collective-permute-start.1 = (f32[16,32,128]{2,1,0:T(8,128)S(1)}, f32[16,32,128]{2,1,0:T(8,128)S(1)}, u32[]{:S(2)}, u32[]{:S(2)}) collective-permute-start(f32[16,32,128]{2,1,0:T(8,128)S(1)} %all-to-all-done.1.ranges.same), channel_id=1, source_target_pairs={{0,1},{1,0},{2,3},{3,2},{4,5},{5,4},{6,7},{7,6},{8,9},{9,8},{10,11... | collective-permute-start | bytes 786440 | tf_op jit(solution)/shard_map/ppermute | solution.py:314
  42.4 3.6 %copy-start.4 = (s32[16,2]{0,1:T(2,128)S(1)}, s32[16,2]{0,1:T(2,128)}, u32[]{:S(2)}) copy-start(s32[16,2]{0,1:T(2,128)} %param.12) | copy-start | bytes 388
  42.4 13.0 %all-to-all-start.2 = ((f32[8,2,32,128]{3,2,1,0:T(8,128)}), f32[8,2,32,128]{3,2,1,0:T(8,128)S(1)}, u32[]{:S(2)}, u32[]{:S(2)}) async-start(f32[8,2,32,128]{3,2,1,0:T(8,128)} %get-tuple-element.22), calls=%async_computation.2 | async-start | bytes 524288 | tf_op jit(solution)/shard_map/all_to_all | solution.py:371
  46.0 0.7 %copy-start.5 = (s32[16,2]{0,1:T(2,128)S(1)}, s32[16,2]{0,1:T(2,128)}, u32[]{:S(2)}) copy-start(s32[16,2]{0,1:T(2,128)} %param.13) | copy-start | bytes 388

commit v2 on v1

--- a/solution.py
+++ b/solution.py
@@ -38,7 +38,9 @@
 def inverse_lower(gram, tasks=()):
     size = gram.shape[0]
     count = size // SUB
-    tasks = list(tasks)
+    due = {}
+    for n, task in enumerate(reversed(tasks)):
+        due.setdefault(max(count - 2 - 2 * n, 0), []).insert(0, task)
     sub_ids = lax.broadcasted_iota(jnp.int32, (SUB, size), 0)
     lane_ids = lax.broadcasted_iota(jnp.int32, (SUB, size), 1)
     rows = [gram[SUB * i : SUB * i + SUB, :] for i in range(count)]
@@ -99,9 +101,8 @@
         kept = jnp.where(lane_ids < SUB * k + SUB, rows[k], 0.0)
         done.append(kept * lax.rsqrt(pivots))
         diag = ahead
-        for task in tasks[: -(-len(tasks) // (count - k))]:
+        for task in due.get(k, ()):
             task()
-        tasks = tasks[-(-len(tasks) // (count - k)) :]
     return jnp.concatenate(done, axis=0)
 
 

time: 56.9 us -> 56.9 us (level)
  no operation moved by 1% of the time
where the time goes in v2:
time: 56.9 us; the launch traced here: 56.4 us
  waiting for transfers between devices  20.8 us (37%)
  starting transfers between devices  17.8 us (31%)
  Pallas kernels  15.6 us (27%)
  local copies, waits for them, and re-layouts  0.78 us (1%)
  between operations  0.75 us (1%)
  other arithmetic  0.71 us (1%)
    all_to_all x1, starting transfers between devices, body(): received = lax.all_to_all(slots, ('gx', 'ay'), 0, 0, tiled=True)  8.16 us
    all_to_all x1, waiting for transfers between devices, body(): received = lax.all_to_all(slots, ('gx', 'ay'), 0, 0, tiled=True)  7.09 us
    all_to_all x1, waiting for transfers between devices, body(): same = lax.all_to_all(copies, ('gx', 'ay'), 0, 0, tiled=True)  6.45 us
    pallas_call x1, Pallas kernels, body(): call(functools.partial(third_kernel, gx, ay, ac, own), [f32((own, rank)),...  4.9 us
    pallas_call x1, Pallas kernels, body(): call(functools.partial(second_kernel, gx, ay, ac), [f32((rank, rank)), f3...  4.64 us
    all_to_all x1, waiting for transfers between devices, body(): every = lax.all_to_all(partial, 'gx', 0, 0, tiled=True)  3.74 us
    all_to_all x1, starting transfers between devices, body(): every = lax.all_to_all(partial, 'gx', 0, 0, tiled=True)  3.57 us
    all_to_all x1, starting transfers between devices, body(): same = lax.all_to_all(copies, ('gx', 'ay'), 0, 0, tiled=True)  3.53 us
  transfers between devices with their start and end apart: 8, of which 5 were waited for; matrix products, arithmetic and copies ran while one was open for 0% of the time, Pallas kernels for 13%

profile of v2, /device:TPU:0, one launch (start us, length us, event | category | flops | bytes accessed | tf_op | source)
XLA Modules:
  0.0 56.4 jit_solution(8147761125137281564)
XLA Ops:
  0.6 0.0 copy-start.2
  0.6 0.0 copy-start.1
  0.7 0.0 copy-start.3
  0.7 0.0 copy-start
  0.7 2.4 %shard_map.94 = (f32[16,24,128]{2,1,0:T(8,128)S(1)}, f32[16,24,128]{2,1,0:T(8,128)S(1)}) custom-call(f32[2,128,512]{2,1,0:T(8,128)} %near_field.1, f32[2,2,256]{2,1,0:T(2,128)} %plane_sketch.1, f32[128,256]{1,0:T(8,128)} %second_in.1, f32[2,256,128]{2,1,0:T(8,128)} %mixing.1), custom_call_target="tpu_custom_call" | custom-call | flops 1000000000 | bytes 1048576 | tf_op jit(solution)/shard_map/pallas_call | solution.py:330
  3.1 0.5 collective-permute-start
  3.6 0.0 copy-done.2
  3.6 0.0 copy-done.1
  3.6 0.0 copy-done.3
  3.6 0.0 copy-done
  3.6 1.1 %shard_map.95 = f32[16,24,128]{2,1,0:T(8,128)S(1)} custom-call(f32[2,128,512]{2,1,0:T(8,128)S(1)} %copy-done.1, f32[2,2,256]{2,1,0:T(2,128)S(1)} %copy-done.3, f32[512,256]{1,0:T(8,128)S(1)} %copy-done, f32[2,256,128]{2,1,0:T(8,128)S(1)} %copy-done.2), custom_call_target="tpu_custom_call" | custom-call | flops 1000000000 | bytes 1048576 | tf_op jit(solution)/shard_map/pallas_call | solution.py:345
  4.7 0.0 collective-permute-done
  4.7 0.7 %add_add_fusion = f32[16,24,128]{2,1,0:T(8,128)} fusion(f32[16,24,128]{2,1,0:T(8,128)S(1)} %collective-permute-done, f32[16,24,128]{2,1,0:T(8,128)S(1)} %get-tuple-element.13, f32[16,24,128]{2,1,0:T(8,128)S(1)} %shard_map.95), kind=kLoop, calls=%fused_computation | loop fusion | flops 98304 | bytes 786432 | tf_op jit(solution)/shard_map/add | solution.py:348
  5.4 8.2 %all-to-all-start = ((f32[16,24,128]{2,1,0:T(8,128)}), f32[16,24,128]{2,1,0:T(8,128)S(1)}, u32[]{:S(2)}, u32[]{:S(2)}) async-start(f32[16,24,128]{2,1,0:T(8,128)} %add_add_fusion), calls=%async_computation | async-start | bytes 393216 | tf_op jit(solution)/shard_map/all_to_all | solution.py:349
  13.6 1.9 %collective-permute-start.3 = (f32[2,128,512]{2,1,0:T(8,128)S(1)}, f32[2,128,512]{2,1,0:T(8,128)S(1)}, u32[]{:S(2)}, u32[]{:S(2)}) collective-permute-start(f32[2,128,512]{2,1,0:T(8,128)S(1)} %copy-done.1), channel_id=1, source_target_pairs={{0,2},{2,0},{1,3},{3,1},{4,6},{6,4},{5,7},{7,5},{8,10},{10,8},{9,1... | collective-permute-start | bytes 1572872 | tf_op jit(solution)/shard_map/ppermute | solution.py:315
  15.5 7.1 %all-to-all-done.received = f32[16,24,128]{2,1,0:T(8,128)S(1)} async-done(((f32[16,24,128]{2,1,0:T(8,128)}), f32[16,24,128]{2,1,0:T(8,128)S(1)}, u32[]{:S(2)}, u32[]{:S(2)}) %all-to-all-start) | async-done | bytes 196640 | tf_op jit(solution)/shard_map/all_to_all | solution.py:349
  22.6 0.7 %shard_map.96 = f32[16,32,128]{2,1,0:T(8,128)} custom-call(f32[16,24,128]{2,1,0:T(8,128)S(1)} %all-to-all-done.received), custom_call_target="tpu_custom_call" | custom-call | flops 1000000 | bytes 1048576 | tf_op jit(solution)/shard_map/pallas_call | solution.py:350
  23.3 3.5 %all-to-all-start.1 = ((f32[16,32,128]{2,1,0:T(8,128)}), f32[16,32,128]{2,1,0:T(8,128)S(1)}, u32[]{:S(2)}, u32[]{:S(2)}) async-start(f32[16,32,128]{2,1,0:T(8,128)} %shard_map.96), calls=%async_computation.1 | async-start | bytes 524288 | tf_op jit(solution)/shard_map/all_to_all | solution.py:356
  26.9 0.1 collective-permute-start.2
  27.0 2.8 %collective-permute-done.3.far_field = f32[2,128,512]{2,1,0:T(8,128)S(1)} collective-permute-done((f32[2,128,512]{2,1,0:T(8,128)S(1)}, f32[2,128,512]{2,1,0:T(8,128)S(1)}, u32[]{:S(2)}, u32[]{:S(2)}) %collective-permute-start.3) | collective-permute-done | bytes 524320 | tf_op jit(solution)/shard_map/ppermute | solution.py:315
  29.8 0.0 collective-permute-start.4
  29.8 6.5 %all-to-all-done.1.ranges.same = f32[16,32,128]{2,1,0:T(8,128)S(1)} async-done(((f32[16,32,128]{2,1,0:T(8,128)}), f32[16,32,128]{2,1,0:T(8,128)S(1)}, u32[]{:S(2)}, u32[]{:S(2)}) %all-to-all-start.1) | async-done | bytes 262176 | tf_op jit(solution)/shard_map/all_to_all | solution.py:356
  36.2 0.0 collective-permute-start.1
  36.2 0.8 %shard_map.97 = (f32[128,1024]{1,0:T(8,128)S(1)}, f32[128,128]{1,0:T(8,128)S(1)}) custom-call(f32[16,32,128]{2,1,0:T(8,128)S(1)} %all-to-all-done.1.ranges.same, f32[2,128,512]{2,1,0:T(8,128)S(1)} %copy-done.1, f32[2,128,512]{2,1,0:T(8,128)S(1)} %collective-permute-done.3.far_field), custom_call_target="tpu_custom_call" | custom-call | flops 1000000000 | bytes 1048576 | tf_op jit(solution)/shard_map/pallas_call | solution.py:359
  37.0 0.0 collective-permute-done.2.near_field
  37.0 0.0 collective-permute-done.4.far_field
  37.0 0.7 %collective-permute-done.1.other = f32[16,32,128]{2,1,0:T(8,128)S(1)} collective-permute-done((f32[16,32,128]{2,1,0:T(8,128)S(1)}, f32[16,32,128]{2,1,0:T(8,128)S(1)}, u32[]{:S(2)}, u32[]{:S(2)}) %collective-permute-start.1) | collective-permute-done | bytes 262176 | tf_op jit(solution)/shard_map/ppermute | solution.py:315
  37.7 4.6 %shard_map.98 = (f32[128,128]{1,0:T(8,128)S(1)}, f32[8,2,32,128]{3,2,1,0:T(8,128)}) custom-call(f32[16,32,128]{2,1,0:T(8,128)S(1)} %all-to-all-done.1.ranges.same, f32[16,32,128]{2,1,0:T(8,128)S(1)} %collective-permute-done.1.other, f32[2,128,512]{2,1,0:T(8,128)S(1)} %collective-permute-done.2.near_field, ...), custom_call_target="tpu_custom_call" | custom-call | flops 2000000000 | bytes 1048576 | tf_op jit(solution)/shard_map/pallas_call | solution.py:365
  42.4 0.0 copy-start.4
  42.4 3.6 %all-to-all-start.2 = ((f32[8,2,32,128]{3,2,1,0:T(8,128)}), f32[8,2,32,128]{3,2,1,0:T(8,128)S(1)}, u32[]{:S(2)}, u32[]{:S(2)}) async-start(f32[8,2,32,128]{3,2,1,0:T(8,128)} %get-tuple-element.22), calls=%async_computation.2 | async-start | bytes 524288 | tf_op jit(solution)/shard_map/all_to_all | solution.py:372
  46.0 0.0 copy-done.4
  46.0 0.0 copy-start.5
  46.0 0.1 copy.10.targets
  46.1 0.6 %copy-done.5 = s32[16,2]{0,1:T(2,128)S(1)} copy-done((s32[16,2]{0,1:T(2,128)S(1)}, s32[16,2]{0,1:T(2,128)}, u32[]{:S(2)}) %copy-start.5) | copy-done | bytes 152
  46.6 0.1 copy.11.signs
  46.7 4.9 %shard_map.99 = (f32[16,128]{1,0:T(8,128)}, f32[16,128]{1,0:T(8,128)}, f32[128,128]{1,0:T(8,128)S(1)}, f32[16,1,128]{2,1,0:T(1,128)S(1)}) custom-call(s32[16,2]{1,0:T(8,128)S(1)} %copy.10.targets, s32[16,2]{1,0:T(8,128)S(1)} %copy.11.signs, f32[16,32,128]{2,1,0:T(8,128)S(1)} %all-to-all-done.1.ranges.same, f32[16,32,128]{2,1,0:T(8,128)S(1)} %collective-permute-done.1.other, ...), custom_call_target="tpu_custom_call" | custom-call | flops 1000000000 | bytes 1048576 | tf_op jit(solution)/shard_map/pallas_call | solution.py:374
  51.6 3.7 %all-to-all-done.2 = f32[8,2,32,128]{3,2,1,0:T(8,128)S(1)} async-done(((f32[8,2,32,128]{3,2,1,0:T(8,128)}), f32[8,2,32,128]{3,2,1,0:T(8,128)S(1)}, u32[]{:S(2)}, u32[]{:S(2)}) %all-to-all-start.2) | async-done | bytes 262176 | tf_op jit(solution)/shard_map/all_to_all | solution.py:372
  55.4 1.1 %shard_map.100 = f32[16,32,128]{2,1,0:T(8,128)} custom-call(f32[16,1,128]{2,1,0:T(1,128)S(1)} %get-tuple-element.20.weights, f32[128,128]{1,0:T(8,128)S(1)} %get-tuple-element.21.turned, f32[16,32,128]{2,1,0:T(8,128)S(1)} %bitcast.1), custom_call_target="tpu_custom_call" | custom-call | flops 100000000 | bytes 1048576 | tf_op jit(solution)/shard_map/pallas_call | solution.py:386
Async XLA Ops:
  0.6 2.9 %copy-start.2 = (f32[2,256,128]{2,1,0:T(8,128)S(1)}, f32[2,256,128]{2,1,0:T(8,128)}, u32[]{:S(2)}) copy-start(f32[2,256,128]{2,1,0:T(8,128)} %mixing.1) | copy-start | bytes 786436
  0.6 2.9 %copy-start.1 = (f32[2,128,512]{2,1,0:T(8,128)S(1)}, f32[2,128,512]{2,1,0:T(8,128)}, u32[]{:S(2)}) copy-start(f32[2,128,512]{2,1,0:T(8,128)} %near_field.1) | copy-start | bytes 1572868
  0.7 2.9 %copy-start.3 = (f32[2,2,256]{2,1,0:T(2,128)S(1)}, f32[2,2,256]{2,1,0:T(2,128)}, u32[]{:S(2)}) copy-start(f32[2,2,256]{2,1,0:T(2,128)} %plane_sketch.1) | copy-start | bytes 12292
  0.7 2.9 %copy-start = (f32[512,256]{1,0:T(8,128)S(1)}, f32[512,256]{1,0:T(8,128)}, u32[]{:S(2)}) copy-start(f32[512,256]{1,0:T(8,128)} %third_sketch.1) | copy-start | bytes 1572868
  3.1 1.7 %collective-permute-start = (f32[16,24,128]{2,1,0:T(8,128)S(1)}, f32[16,24,128]{2,1,0:T(8,128)S(1)}, u32[]{:S(2)}, u32[]{:S(2)}) collective-permute-start(f32[16,24,128]{2,1,0:T(8,128)S(1)} %get-tuple-element.14), channel_id=1, source_target_pairs={{0,1},{1,0},{2,3},{3,2},{4,5},{5,4},{6,7},{7,6},{8,9},{9,8},{10,11... | collective-permute-start | bytes 589832 | tf_op jit(solution)/shard_map/ppermute | solution.py:315
  5.4 17.2 %all-to-all-start = ((f32[16,24,128]{2,1,0:T(8,128)}), f32[16,24,128]{2,1,0:T(8,128)S(1)}, u32[]{:S(2)}, u32[]{:S(2)}) async-start(f32[16,24,128]{2,1,0:T(8,128)} %add_add_fusion), calls=%async_computation | async-start | bytes 393216 | tf_op jit(solution)/shard_map/all_to_all | solution.py:349
  13.6 16.2 %collective-permute-start.3 = (f32[2,128,512]{2,1,0:T(8,128)S(1)}, f32[2,128,512]{2,1,0:T(8,128)S(1)}, u32[]{:S(2)}, u32[]{:S(2)}) collective-permute-start(f32[2,128,512]{2,1,0:T(8,128)S(1)} %copy-done.1), channel_id=1, source_target_pairs={{0,2},{2,0},{1,3},{3,1},{4,6},{6,4},{5,7},{7,5},{8,10},{10,8},{9,1... | collective-permute-start | bytes 1572872 | tf_op jit(solution)/shard_map/ppermute | solution.py:315
  23.3 12.9 %all-to-all-start.1 = ((f32[16,32,128]{2,1,0:T(8,128)}), f32[16,32,128]{2,1,0:T(8,128)S(1)}, u32[]{:S(2)}, u32[]{:S(2)}) async-start(f32[16,32,128]{2,1,0:T(8,128)} %shard_map.96), calls=%async_computation.1 | async-start | bytes 524288 | tf_op jit(solution)/shard_map/all_to_all | solution.py:356
  26.9 10.1 %collective-permute-start.2 = (f32[2,128,512]{2,1,0:T(8,128)S(1)}, f32[2,128,512]{2,1,0:T(8,128)S(1)}, u32[]{:S(2)}, u32[]{:S(2)}) collective-permute-start(f32[2,128,512]{2,1,0:T(8,128)S(1)} %copy-done.1), channel_id=1, source_target_pairs={{0,1},{1,0},{2,3},{3,2},{4,5},{5,4},{6,7},{7,6},{8,9},{9,8},{10,11... | collective-permute-start | bytes 1572872 | tf_op jit(solution)/shard_map/ppermute | solution.py:315
  29.8 7.2 %collective-permute-start.4 = (f32[2,128,512]{2,1,0:T(8,128)S(1)}, f32[2,128,512]{2,1,0:T(8,128)S(1)}, u32[]{:S(2)}, u32[]{:S(2)}) collective-permute-start(f32[2,128,512]{2,1,0:T(8,128)S(1)} %collective-permute-done.3.far_field), channel_id=1, source_target_pairs={{0,1},{1,0},{2,3},{3,2},{4,5},{5,4},{6,7},{7,6},{8,9},{9,8},{10,11... | collective-permute-start | bytes 1572872 | tf_op jit(solution)/shard_map/ppermute | solution.py:315
  36.2 1.5 %collective-permute-start.1 = (f32[16,32,128]{2,1,0:T(8,128)S(1)}, f32[16,32,128]{2,1,0:T(8,128)S(1)}, u32[]{:S(2)}, u32[]{:S(2)}) collective-permute-start(f32[16,32,128]{2,1,0:T(8,128)S(1)} %all-to-all-done.1.ranges.same), channel_id=1, source_target_pairs={{0,1},{1,0},{2,3},{3,2},{4,5},{5,4},{6,7},{7,6},{8,9},{9,8},{10,11... | collective-permute-start | bytes 786440 | tf_op jit(solution)/shard_map/ppermute | solution.py:315
  42.4 3.6 %copy-start.4 = (s32[16,2]{0,1:T(2,128)S(1)}, s32[16,2]{0,1:T(2,128)}, u32[]{:S(2)}) copy-start(s32[16,2]{0,1:T(2,128)} %param.12) | copy-start | bytes 388
  42.4 13.0 %all-to-all-start.2 = ((f32[8,2,32,128]{3,2,1,0:T(8,128)}), f32[8,2,32,128]{3,2,1,0:T(8,128)S(1)}, u32[]{:S(2)}, u32[]{:S(2)}) async-start(f32[8,2,32,128]{3,2,1,0:T(8,128)} %get-tuple-element.22), calls=%async_computation.2 | async-start | bytes 524288 | tf_op jit(solution)/shard_map/all_to_all | solution.py:372
  46.0 0.7 %copy-start.5 = (s32[16,2]{0,1:T(2,128)S(1)}, s32[16,2]{0,1:T(2,128)}, u32[]{:S(2)}) copy-start(s32[16,2]{0,1:T(2,128)} %param.13) | copy-start | bytes 388
